TPU v7x, 256 devices: a whole 4x4x8 slice. The times are simulated.
256 devices in a mesh: ex: 16 (over x_hi, y, core), mat: 16 (over x_lo, z).
Axes of the slice: x: 4 (x_hi: 2, x_lo: 2; x = x_hi * 2 + x_lo), y: 4, z: 8, core: 2. Of those that a mesh axis runs over, the one named last changes fastest.
Arguments:
- train_grads: bfloat16 [16384, 16, 2048], P(('ex', 'mat')), may hold values from -6 to 6
- inverse_hessian: bfloat16 [16, 2048, 2048], P('mat'), as said below
- query_grads: bfloat16 [256, 16, 2048], P('ex', 'mat'), may hold values from -0.046875 to 0.046875
Outputs:
- preconditioned: bfloat16 [16384, 16, 2048], P('ex', 'mat')
- scores: float32 [256, 16384], P('mat', 'ex')
Inputs may be any that keep to these rules, and one draw needn't show every extreme that they name: `inverse_hessian`: each matrix is its diagonal plus full-rank terms off it.
All inputs are finite; a program needn't handle non-finite values.
Results may differ from a plain program's by a relative error of at most 0.0029.
Values may be sent and summed in bfloat16 or wider, within the bound.
A program may use at most 128 MiB of HBM per device.

v0:
```python
import jax
import jax.numpy as jnp
from jax import lax
from jax.sharding import PartitionSpec as P


def on_device(train_grads, inverse_hessian, query_grads):
    regrouped = lax.all_to_all(train_grads, "mat", split_axis=1, concat_axis=0, tiled=True)
    product = jnp.einsum(
        "rmk,mkj->rmj", regrouped, inverse_hessian, preferred_element_type=jnp.float32
    )
    preconditioned = product.astype(jnp.bfloat16)
    partial_scores = jnp.einsum(
        "qmk,rmk->qr",
        lax.all_gather(query_grads, "ex", axis=0, tiled=True),
        preconditioned,
        preferred_element_type=jnp.float32,
    )
    scores = lax.psum_scatter(partial_scores, "mat", scatter_dimension=0, tiled=True)
    return (preconditioned, scores)


def solution(mesh):
    return jax.shard_map(
        on_device,
        mesh=mesh,
        in_specs=(P(("ex", "mat"), None, None), P("mat", None, None), P("ex", "mat", None)),
        out_specs=(P("ex", "mat", None), P("mat", "ex")),
        check_vma=False,
    )
```

profile of v0, /device:TPU:8, one launch (start us, length us, event | category | flops | bytes accessed | tf_op | source)
XLA Modules:
  0.0 216.4 jit_solution(13022691823905977757)
XLA Ops:
  7.2 6.5 %copy.10 = bf16[64,16,2048]{2,0,1:T(8,128)(2,1)} copy(bf16[64,16,2048]{2,1,0:T(8,128)(2,1)} %param.3) | data formatting | bytes 8388608 | tf_op args[0]
  13.7 9.5 %all-to-all-start = ((bf16[64,16,2048]{2,0,1:T(8,128)(2,1)}), bf16[64,16,2048]{2,0,1:T(8,128)(2,1)}, u32[]{:S(2)}, u32[]{:S(2)}) async-start(bf16[64,16,2048]{2,0,1:T(8,128)(2,1)} %copy.10), calls=%async_computation | async-start | bytes 8388608 | tf_op jit(solution)/shard_map/all_to_all | solution.py:8
  23.2 0.0 all-gather.2.cloned.1.call-start
  23.3 0.7 all-gather.2.cloned.1.call-update
  24.0 0.0 reduce-scatter.4.cloned.1.call-start
  24.0 94.4 %all-to-all-done = bf16[64,16,2048]{2,0,1:T(8,128)(2,1)} async-done(((bf16[64,16,2048]{2,0,1:T(8,128)(2,1)}), bf16[64,16,2048]{2,0,1:T(8,128)(2,1)}, u32[]{:S(2)}, u32[]{:S(2)}) %all-to-all-start) | async-done | bytes 4194336 | tf_op jit(solution)/shard_map/all_to_all | solution.py:8
  118.4 13.9 %fusion.4 = bf16[2048,1024]{1,0:T(8,128)(2,1)} fusion(bf16[1024,2048]{1,0:T(8,128)(2,1)} %bitcast.3, bf16[1,2048,2048]{2,1,0:T(8,128)(2,1)} %param.4), kind=kOutput, calls=%fused_computation.4 | convolution fusion | flops 8592031744 | bytes 16777216 | tf_op jit(solution)/shard_map/rmk,mkj->rmj/dot_general | solution.py:9
  132.3 0.0 all-gather.2.cloned.1.call-done
  132.3 3.8 %fusion.7 = f32[256,1024]{0,1:T(8,128)S(1)} fusion(bf16[2048,1024]{1,0:T(8,128)(2,1)} %fusion.4, bf16[256,1,2048]{2,0,1:T(8,128)(2,1)} %all-gather.2.cloned.1.call-done), kind=kOutput, calls=%fused_computation.5 | convolution fusion | flops 1073741824 | bytes 6291456 | tf_op jit(solution)/shard_map/qmk,rmk->qr/dot_general | solution.py:13
  136.1 1.3 copy.13
  137.4 0.0 reduce-scatter.4.cloned.1.call-update
  137.4 6.4 %copy.11 = bf16[1024,1,2048]{2,0,1:T(8,128)(2,1)} copy(bf16[1024,1,2048]{0,2,1:T(8,128)(2,1)} %bitcast.26) | data formatting | bytes 8388608
  143.9 65.7 %reduce-scatter.4.cloned.1.call-done = f32[16,1024]{1,0:T(8,128)} async-done(((f32[256,1024]{1,0:T(8,128)}), f32[16,1024]{1,0:T(8,128)}) %reduce-scatter.4.cloned.1.call-update) | async-done | bytes 65552
Async XLA Ops:
  13.7 104.8 %all-to-all-start = ((bf16[64,16,2048]{2,0,1:T(8,128)(2,1)}), bf16[64,16,2048]{2,0,1:T(8,128)(2,1)}, u32[]{:S(2)}, u32[]{:S(2)}) async-start(bf16[64,16,2048]{2,0,1:T(8,128)(2,1)} %copy.10), calls=%async_computation | async-start | bytes 8388608 | tf_op jit(solution)/shard_map/all_to_all | solution.py:8
  23.2 109.1 %all-gather.2.cloned.1.call-start = ((), (), s32[]{:S(2)}) async-start(), calls=%async_computation.2 | async-start | bytes 1114112 | tf_op jit(solution)/shard_map/all_gather | solution.py:15
  24.0 185.6 %reduce-scatter.4.cloned.1.call-start = ((), (), s32[]{:S(2)}) async-start(), calls=%async_computation.3 | async-start | bytes 1114112
Sparse Core Ops, SparseCore 0:
  26.8 62.2 all-gather.1
  137.6 71.9 reduce-scatter.3
where the time goes:
time: 217 us; the launch traced here: 216 us
  waiting for transfers between devices  161 us (74%)
  matrix products  17.7 us (8%)
  local copies, waits for them, and re-layouts  14.2 us (7%)
  between operations  14.1 us (6%)
  starting transfers between devices  9.63 us (4%)
    all_to_all x1, waiting for transfers between devices, on_device(): lax.all_to_all(train_grads, 'mat', split_axis=1, concat_axis=0, tiled=True)  94.4 us
    unnamed x3, waiting for transfers between devices  66.4 us
    unnamed x3, local copies, waits for them, and re-layouts  14.2 us
    dot_general x1, matrix products, on_device(): jnp.einsum('rmk,mkj->rmj', regrouped, inverse_hessian, preferred_element_...  13.9 us
    all_to_all x1, starting transfers between devices, on_device(): lax.all_to_all(train_grads, 'mat', split_axis=1, concat_axis=0, tiled=True)  9.55 us
  transfers between devices with their start and end apart: 3, of which 2 were waited for; matrix products, arithmetic and copies ran while one was open for 9% of the time, Pallas kernels for 0%

commit v1 on v0

v1 whole, which is shorter than its diff:
```python
import functools

import jax
import jax.numpy as jnp
from jax import lax
from jax.experimental import pallas as pl
from jax.experimental.pallas import tpu as pltpu
from jax.sharding import PartitionSpec as P

MESH = pl.DeviceIdType.MESH
F32, BF16 = jnp.float32, jnp.bfloat16
GROUPS = 4
ZS = 8
TILE = 512

PEERS = (
    (0, 4), (1, 4), (0, 3), (0, 5), (1, 3), (1, 5), (0, 2), (0, 6),
    (1, 2), (1, 6), (0, 1), (0, 7), (1, 1), (1, 7), (1, 0),
)


def peer(me, offset, sign):
    dx, dz = offset
    x, z = me // ZS, lax.rem(me, ZS)
    return lax.rem(x + dx, 2) * ZS + lax.rem(z + (dz if sign > 0 else ZS - dz), ZS)


def kernel(
    n_ex,
    n_mat,
    train_ref,
    hess_ref,
    query_ref,
    pre_ref,
    scores_ref,
    staged,
    outgoing,
    arrived,
    hess,
    queries,
    pre,
    terms,
    terms_in,
    load_sem,
    hess_sem,
    query_load_sem,
    send_sem,
    recv_sem,
    query_send_sem,
    query_recv_sem,
    term_send_sem,
    term_recv_sem,
    out_sem,
):
    me = lax.axis_index("mat")
    my_ex = lax.axis_index("ex")
    group_rows = train_ref.shape[0] // GROUPS
    part = group_rows // n_mat
    columns = train_ref.shape[1]

    def load(g):
        rows = pl.ds(g * group_rows, group_rows)
        return pltpu.make_async_copy(train_ref.at[rows], staged.at[g], load_sem.at[g])

    my_queries = pl.ds(pl.multiple_of(my_ex * 16, 16), 16)
    query_load = pltpu.make_async_copy(query_ref, queries.at[my_queries], query_load_sem)
    hess_load = pltpu.make_async_copy(hess_ref, hess, hess_sem)

    for g in range(GROUPS):
        load(g).start()
    query_load.start()
    hess_load.start()

    barrier = pltpu.get_barrier_semaphore()
    for k in range(1, n_mat):
        pl.semaphore_signal(
            barrier, inc=1, device_id={"mat": lax.rem(me + k, n_mat)}, device_id_type=MESH
        )
    for k in range(1, n_ex):
        pl.semaphore_signal(
            barrier, inc=1, device_id={"ex": lax.rem(my_ex + k, n_ex)}, device_id_type=MESH
        )

    out_row = lax.broadcasted_iota(jnp.int32, (group_rows, group_rows), 0)
    in_row = lax.broadcasted_iota(jnp.int32, (group_rows, group_rows), 1)
    regroup = jnp.where(
        in_row == lax.rem(out_row, part) * n_mat + out_row // part, 1.0, 0.0
    ).astype(BF16)
    mine = pl.ds(pl.multiple_of(me * part, part), part)

    def regroup_rows(g):
        load(g).wait()
        for c in range(columns // TILE):
            cols = pl.ds(c * TILE, TILE)
            outgoing[g, :, cols] = jnp.dot(
                regroup, staged[g, :, cols], preferred_element_type=F32
            ).astype(BF16)
        arrived[g, mine, :] = outgoing[g, mine, :]

    def send(g, i):
        to = peer(me, PEERS[i], 1)
        return pltpu.make_async_remote_copy(
            src_ref=outgoing.at[g, pl.ds(pl.multiple_of(to * part, part), part)],
            dst_ref=arrived.at[g, mine],
            send_sem=send_sem.at[g, i],
            recv_sem=recv_sem.at[g, i],
            device_id={"mat": to},
            device_id_type=MESH,
        )

    def arrival(g, i):
        source = peer(me, PEERS[i], -1)
        rows = pl.ds(pl.multiple_of(source * part, part), part)
        return pltpu.make_async_remote_copy(
            src_ref=outgoing.at[g, rows],
            dst_ref=arrived.at[g, rows],
            send_sem=send_sem.at[g, i],
            recv_sem=recv_sem.at[g, i],
            device_id={"mat": source},
            device_id_type=MESH,
        )

    def query_send(k):
        return pltpu.make_async_remote_copy(
            src_ref=queries.at[my_queries],
            dst_ref=queries.at[my_queries],
            send_sem=query_send_sem.at[k],
            recv_sem=query_recv_sem.at[k],
            device_id={"ex": lax.rem(my_ex + k, n_ex)},
            device_id_type=MESH,
        )

    def query_arrival(k):
        source = lax.rem(my_ex + n_ex - k, n_ex)
        rows = pl.ds(pl.multiple_of(source * 16, 16), 16)
        return pltpu.make_async_remote_copy(
            src_ref=queries.at[rows],
            dst_ref=queries.at[rows],
            send_sem=query_send_sem.at[k],
            recv_sem=query_recv_sem.at[k],
            device_id={"ex": source},
            device_id_type=MESH,
        )

    def term_send(g, i):
        to = peer(me, PEERS[i], 1)
        return pltpu.make_async_remote_copy(
            src_ref=terms.at[g, pl.ds(pl.multiple_of(to * 16, 16), 16)],
            dst_ref=terms_in.at[g, i + 1],
            send_sem=term_send_sem.at[g, i],
            recv_sem=term_recv_sem.at[g, i],
            device_id={"mat": to},
            device_id_type=MESH,
        )

    def out_copy(g, k):
        rows = pl.ds(pl.multiple_of(k * (part * GROUPS) + g * part, part), part)
        return pltpu.make_async_copy(
            pre.at[g, pl.ds(k * part, part)], pre_ref.at[rows], out_sem.at[g, k]
        )

    regroup_rows(0)
    query_load.wait()
    pl.semaphore_wait(barrier, n_mat + n_ex - 2)
    for i in range(len(PEERS)):
        send(0, i).start()
    for k in range(1, n_ex):
        query_send(k).start()
    regroup_rows(1)
    for i in range(len(PEERS)):
        send(1, i).start()
    for g in range(2, GROUPS):
        regroup_rows(g)

    my_terms = pl.ds(pl.multiple_of(me * 16, 16), 16)
    for g in range(GROUPS):
        for i in range(len(PEERS)):
            arrival(g, i).wait_recv()
        if g + 2 < GROUPS:
            for i in range(len(PEERS)):
                send(g + 2, i).start()
        if g == 0:
            hess_load.wait()

        def multiply(c, carry, g=g):
            cols = pl.ds(pl.multiple_of(c * TILE, TILE), TILE)
            pre[g, :, cols] = jnp.dot(
                arrived[g], hess[:, cols], preferred_element_type=F32
            ).astype(BF16)
            return carry

        lax.fori_loop(0, columns // TILE, multiply, 0)
        for k in range(n_mat):
            out_copy(g, k).start()
        if g == 0:
            for k in range(1, n_ex):
                query_arrival(k).wait_recv()
        terms[g] = lax.dot_general(
            queries[...], pre[g], (((1,), (1,)), ((), ())), preferred_element_type=F32
        ).astype(BF16)
        for i in range(len(PEERS)):
            term_send(g, i).start()
        terms_in[g, 0] = terms[g, my_terms, :]

    lane = lax.broadcasted_iota(jnp.int32, (16, 128), 1)
    totals = []
    for g in range(GROUPS):
        for i in range(len(PEERS)):
            term_send(g, i).wait_recv()
        total = terms_in[g, 0].astype(F32)
        for i in range(len(PEERS)):
            total += terms_in[g, i + 1].astype(F32)
        totals.append(total)
    for j in range(scores_ref.shape[1] // 128):
        tile = jnp.zeros((16, 128), F32)
        for s in range(2):
            source = 2 * j + s
            at, of = (source * part) % 128, source * part // 128
            for g in range(GROUPS):
                to = s * 64 + g * part
                moved = pltpu.roll(totals[g][:, of * 128 : of * 128 + 128], (to - at) % 128, 1)
                tile = jnp.where((lane >= to) & (lane < to + part), moved, tile)
        scores_ref[:, j * 128 : j * 128 + 128] = tile

    for g in range(GROUPS):
        for i in range(len(PEERS)):
            send(g, i).wait_send()
            term_send(g, i).wait_send()
        for k in range(n_mat):
            out_copy(g, k).wait()
    for k in range(1, n_ex):
        query_send(k).wait_send()


def on_device(n_ex, n_mat, train_grads, inverse_hessian, query_grads):
    rows, mats, columns = train_grads.shape
    all_rows = rows * mats
    group_rows = all_rows // GROUPS
    n_queries = query_grads.shape[0] * n_ex
    dma = pltpu.SemaphoreType.DMA
    pre, scores = pl.pallas_call(
        functools.partial(kernel, n_ex, n_mat),
        name="influence",
        out_shape=(
            jax.ShapeDtypeStruct((all_rows, columns), BF16),
            jax.ShapeDtypeStruct((n_queries // n_mat, all_rows), F32),
        ),
        in_specs=[pl.BlockSpec(memory_space=pl.ANY)] * 3,
        out_specs=(
            pl.BlockSpec(memory_space=pl.ANY),
            pl.BlockSpec(memory_space=pltpu.VMEM),
        ),
        scratch_shapes=[
            pltpu.VMEM((GROUPS, group_rows, columns), BF16),
            pltpu.VMEM((GROUPS, group_rows, columns), BF16),
            pltpu.VMEM((GROUPS, group_rows, columns), BF16),
            pltpu.VMEM((columns, columns), BF16),
            pltpu.VMEM((n_queries, columns), BF16),
            pltpu.VMEM((GROUPS, group_rows, columns), BF16),
            pltpu.VMEM((GROUPS, n_queries, group_rows), BF16),
            pltpu.VMEM((GROUPS, n_mat, n_queries // n_mat, group_rows), BF16),
            dma((GROUPS,)),
            dma,
            dma,
            dma((GROUPS, n_mat)),
            dma((GROUPS, n_mat)),
            dma((n_ex,)),
            dma((n_ex,)),
            dma((GROUPS, n_mat)),
            dma((GROUPS, n_mat)),
            dma((GROUPS, n_mat)),
        ],
        compiler_params=pltpu.CompilerParams(
            collective_id=0, has_side_effects=True, vmem_limit_bytes=56 * 2**20
        ),
        cost_estimate=pl.CostEstimate(
            flops=2 * all_rows * columns * (columns + n_queries),
            bytes_accessed=2 * columns * (2 * all_rows + columns),
            transcendentals=0,
        ),
    )(
        train_grads.reshape(all_rows, columns),
        inverse_hessian.reshape(columns, columns),
        query_grads.reshape(query_grads.shape[0], columns),
    )
    return pre.reshape(all_rows, 1, columns), scores


def solution(mesh):
    return jax.shard_map(
        functools.partial(on_device, mesh.shape["ex"], mesh.shape["mat"]),
        mesh=mesh,
        in_specs=(P(("ex", "mat"), None, None), P("mat", None, None), P("ex", "mat", None)),
        out_specs=(P("ex", "mat", None), P("mat", "ex")),
        check_vma=False,
    )
```

time: 217 us -> 125 us (0.58)
  waiting for transfers between devices: 161 us -> 0 us
  Pallas kernels: 0 us -> 119 us
  matrix products: 17.7 us -> 0 us
  between operations: 14.1 us -> 0.65 us
  starting transfers between devices: 9.63 us -> 0 us
  local copies, waits for them, and re-layouts: 14.2 us -> 5.45 us
    pallas_call x0 -> x1, Pallas kernels: none -> 119 us  [on_device(): pl.pallas_call(functools.partial(kernel, n_ex, n_mat), name='influence',...]
    all_to_all x1 -> x0, waiting for transfers between devices: 94.4 us -> none  [on_device(): lax.all_to_all(train_grads, 'mat', split_axis=1, concat_axis=0, tiled=True)]
    unnamed x3 -> x0, waiting for transfers between devices: 66.4 us -> none
    dot_general x2 -> x0, matrix products: 17.7 us -> none  [the longest x1 13.9 us: on_device(): jnp.einsum('rmk,mkj->rmj', regrouped, inverse_hessian, preferred_element_...]
    all_to_all x1 -> x0, starting transfers between devices: 9.55 us -> none  [on_device(): lax.all_to_all(train_grads, 'mat', split_axis=1, concat_axis=0, tiled=True)]
    unnamed x3 -> x4, local copies, waits for them, and re-layouts: 14.2 us -> 5.45 us
  transfers between devices with their start and end apart: 3 -> 0, of which waited for: 2 -> 0; matrix products, arithmetic and copies ran while one was open for 9% -> 0% of each run, Pallas kernels for 0% -> 0%
where the time goes in v1:
time: 125 us
  Pallas kernels  119 us (95%)
  local copies, waits for them, and re-layouts  5.45 us (4%)
    pallas_call x1, Pallas kernels, on_device(): pl.pallas_call(functools.partial(kernel, n_ex, n_mat), name='influence',...  119 us
    unnamed x4, local copies, waits for them, and re-layouts  5.45 us

profile of v1, /device:TPU:8, one launch (start us, length us, event | category | flops | bytes accessed | tf_op | source)
XLA Modules:
  0.0 125.3 jit_solution(3573026647791685385)
XLA Ops:
  0.6 119.2 %influence.1 = (bf16[1024,2048]{1,0:T(8,128)(2,1)}, f32[16,1024]{1,0:T(8,128)}) custom-call(bf16[1024,2048]{1,0:T(8,128)(2,1)} %bitcast.6, bf16[2048,2048]{1,0:T(8,128)(2,1)} %bitcast.5, bf16[16,2048]{1,0:T(8,128)(2,1)} %bitcast.7), custom_call_target="tpu_custom_call" | custom-call | flops 9663676416 | bytes 16777216 | tf_op jit(solution)/shard_map/influence/pallas_call | solution.py:241
  119.8 0.0 copy-start
  119.8 4.8 %copy.7 = bf16[1024,1,2048]{2,0,1:T(8,128)(2,1)} copy(bf16[1024,1,2048]{2,0,1:T(8,128)(2,1)} %bitcast.4) | data formatting | bytes 8388608
  124.6 0.0 copy-done
  124.7 0.6 copy.8
Async XLA Ops:
  119.8 4.8 %copy-start = (f32[16,1024]{1,0:T(8,128)S(1)}, f32[16,1024]{1,0:T(8,128)}, u32[]{:S(2)}) copy-start(f32[16,1024]{1,0:T(8,128)} %get-tuple-element.9) | copy-start | bytes 196612

commit v2 on v1

--- a/solution.py
+++ b/solution.py
@@ -12,6 +12,9 @@
 GROUPS = 4
 ZS = 8
 TILE = 512
+WIDE = 1024
+AHEAD = 8
+PASS_AT = 11
 
 PEERS = (
     (0, 4), (1, 4), (0, 3), (0, 5), (1, 3), (1, 5), (0, 2), (0, 6),
@@ -38,9 +41,15 @@
     arrived,
     hess,
     queries,
-    pre,
+    carried,
     terms,
-    terms_in,
+    own,
+    x_out,
+    x_in,
+    z_out,
+    z_in,
+    last_out,
+    last_in,
     load_sem,
     hess_sem,
     query_load_sem,
@@ -48,15 +57,20 @@
     recv_sem,
     query_send_sem,
     query_recv_sem,
+    x_send_sem,
+    x_recv_sem,
+    z_send_sem,
+    z_recv_sem,
     term_send_sem,
     term_recv_sem,
-    out_sem,
 ):
     me = lax.axis_index("mat")
     my_ex = lax.axis_index("ex")
     group_rows = train_ref.shape[0] // GROUPS
     part = group_rows // n_mat
     columns = train_ref.shape[1]
+    n_queries = queries.shape[0]
+    share = n_queries // n_mat
 
     def load(g):
         rows = pl.ds(g * group_rows, group_rows)
@@ -142,94 +156,152 @@
             device_id_type=MESH,
         )
 
-    def term_send(g, i):
+    def x_copy(g):
+        return pltpu.make_async_remote_copy(
+            src_ref=x_out.at[g],
+            dst_ref=x_in.at[g],
+            send_sem=x_send_sem.at[g],
+            recv_sem=x_recv_sem.at[g],
+            device_id={"mat": peer(me, (1, 0), 1)},
+            device_id_type=MESH,
+        )
+
+    def z_copy(g, k):
+        to = peer(me, (0, k), 1)
+        return pltpu.make_async_remote_copy(
+            src_ref=z_out.at[g, pl.ds(pl.multiple_of(lax.rem(to, ZS) * share, share), share)],
+            dst_ref=z_in.at[g, k],
+            send_sem=z_send_sem.at[g, k],
+            recv_sem=z_recv_sem.at[g, k],
+            device_id={"mat": to},
+            device_id_type=MESH,
+        )
+
+    def term_copy(i):
         to = peer(me, PEERS[i], 1)
         return pltpu.make_async_remote_copy(
-            src_ref=terms.at[g, pl.ds(pl.multiple_of(to * 16, 16), 16)],
-            dst_ref=terms_in.at[g, i + 1],
-            send_sem=term_send_sem.at[g, i],
-            recv_sem=term_recv_sem.at[g, i],
+            src_ref=last_out.at[pl.ds(pl.multiple_of(to * share, share), share)],
+            dst_ref=last_in.at[i],
+            send_sem=term_send_sem.at[i],
+            recv_sem=term_recv_sem.at[i],
             device_id={"mat": to},
             device_id_type=MESH,
         )
 
-    def out_copy(g, k):
-        rows = pl.ds(pl.multiple_of(k * (part * GROUPS) + g * part, part), part)
-        return pltpu.make_async_copy(
-            pre.at[g, pl.ds(k * part, part)], pre_ref.at[rows], out_sem.at[g, k]
-        )
+    n_peers = len(PEERS)
+    order = [(g, i) for g in range(GROUPS) for i in range(n_peers)]
+    side, place = me // ZS, lax.rem(me, ZS)
+    half = n_queries // 2
+    my_half = pl.ds(pl.multiple_of(side * half, half), half)
+    other_half = pl.ds(pl.multiple_of((1 - side) * half, half), half)
+    my_share = pl.ds(pl.multiple_of(place * share, share), share)
+    my_terms = pl.ds(pl.multiple_of(me * share, share), share)
+
+    def multiply(g):
+        def tile(c, carry):
+            cols = pl.ds(pl.multiple_of(c * WIDE, WIDE), WIDE)
+            product = jnp.dot(arrived[g], hess[:, cols], preferred_element_type=F32)
+            pre_ref[:, pl.ds(g * part, part), cols] = product.astype(BF16).reshape(
+                n_mat, part, WIDE
+            )
+            return carry
+
+        lax.fori_loop(0, columns // WIDE, tile, 0)
+
+    def scores_of(left, rows):
+        return lax.dot_general(left, rows, (((1,), (1,)), ((), ())), preferred_element_type=F32)
+
+    def start_terms(g):
+        rows = pre_ref[:, pl.ds(g * part, part), :].reshape(group_rows, columns)
+        terms[...] = scores_of(queries[...], rows)
+        x_out[g] = terms[other_half, :].astype(BF16)
+        x_copy(g).start()
+
+    def pass_terms(g):
+        x_copy(g).wait_recv()
+        terms[my_half, :] = terms[my_half, :] + x_in[g].astype(F32)
+        z_out[g] = terms[my_half, :].astype(BF16)
+        for k in (4, 3, 5, 2, 6, 1, 7):
+            z_copy(g, k).start()
+        own[g] = terms[my_terms, :]
+
+    lane = lax.broadcasted_iota(jnp.int32, (share, 128), 1)
+
+    def place_scores(g, total):
+        for j in range(scores_ref.shape[1] // 128):
+            cols = pl.ds(j * 128, 128)
+            tile = scores_ref[:, cols]
+            for s in range(2):
+                at, of = ((2 * j + s) * part) % 128, (2 * j + s) * part // 128
+                to = s * (part * GROUPS) + g * part
+                moved = pltpu.roll(total[:, of * 128 : of * 128 + 128], (to - at) % 128, 1)
+                tile = jnp.where((lane >= to) & (lane < to + part), moved, tile)
+            scores_ref[:, cols] = tile
 
     regroup_rows(0)
     query_load.wait()
     pl.semaphore_wait(barrier, n_mat + n_ex - 2)
-    for i in range(len(PEERS)):
-        send(0, i).start()
+    for j in range(AHEAD):
+        send(*order[j]).start()
     for k in range(1, n_ex):
         query_send(k).start()
-    regroup_rows(1)
-    for i in range(len(PEERS)):
-        send(1, i).start()
-    for g in range(2, GROUPS):
+    for g in range(1, GROUPS):
         regroup_rows(g)
-
-    my_terms = pl.ds(pl.multiple_of(me * 16, 16), 16)
-    for g in range(GROUPS):
-        for i in range(len(PEERS)):
-            arrival(g, i).wait_recv()
-        if g + 2 < GROUPS:
-            for i in range(len(PEERS)):
-                send(g + 2, i).start()
-        if g == 0:
-            hess_load.wait()
-
-        def multiply(c, carry, g=g):
-            cols = pl.ds(pl.multiple_of(c * TILE, TILE), TILE)
-            pre[g, :, cols] = jnp.dot(
-                arrived[g], hess[:, cols], preferred_element_type=F32
-            ).astype(BF16)
-            return carry
-
-        lax.fori_loop(0, columns // TILE, multiply, 0)
-        for k in range(n_mat):
-            out_copy(g, k).start()
-        if g == 0:
-            for k in range(1, n_ex):
-                query_arrival(k).wait_recv()
-        terms[g] = lax.dot_general(
-            queries[...], pre[g], (((1,), (1,)), ((), ())), preferred_element_type=F32
-        ).astype(BF16)
-        for i in range(len(PEERS)):
-            term_send(g, i).start()
-        terms_in[g, 0] = terms[g, my_terms, :]
-
-    lane = lax.broadcasted_iota(jnp.int32, (16, 128), 1)
-    totals = []
-    for g in range(GROUPS):
-        for i in range(len(PEERS)):
-            term_send(g, i).wait_recv()
-        total = terms_in[g, 0].astype(F32)
-        for i in range(len(PEERS)):
-            total += terms_in[g, i + 1].astype(F32)
-        totals.append(total)
-    for j in range(scores_ref.shape[1] // 128):
-        tile = jnp.zeros((16, 128), F32)
-        for s in range(2):
-            source = 2 * j + s
-            at, of = (source * part) % 128, source * part // 128
-            for g in range(GROUPS):
-                to = s * 64 + g * part
-                moved = pltpu.roll(totals[g][:, of * 128 : of * 128 + 128], (to - at) % 128, 1)
-                tile = jnp.where((lane >= to) & (lane < to + part), moved, tile)
-        scores_ref[:, j * 128 : j * 128 + 128] = tile
-
-    for g in range(GROUPS):
-        for i in range(len(PEERS)):
-            send(g, i).wait_send()
-            term_send(g, i).wait_send()
-        for k in range(n_mat):
-            out_copy(g, k).wait()
+    scores_ref[...] = jnp.zeros_like(scores_ref)
+    hess_load.wait()
+    for k in range(1, n_ex):
+        query_arrival(k).wait_recv()
+
+    for j, (g, i) in enumerate(order):
+        arrival(g, i).wait_recv()
+        if j + AHEAD < len(order):
+            send(*order[j + AHEAD]).start()
+        if i == PASS_AT and g > 0:
+            pass_terms(g - 1)
+        if i == 3 and g == 1:
+
+            def carry_back(c, carry):
+                cols = pl.ds(pl.multiple_of(c * TILE, TILE), TILE)
+                carried[:, cols] = scores_of(queries[...], hess[cols, :]).astype(BF16)
+                return carry
+
+            lax.fori_loop(0, columns // TILE, carry_back, 0)
+        if i == n_peers - 1 and g < GROUPS - 1:
+            multiply(g)
+            start_terms(g)
+
+    last = GROUPS - 1
+    terms[...] = scores_of(carried[...], arrived[last])
+    last_out[...] = terms[...].astype(BF16)
+    for i in range(n_peers):
+        term_copy(i).start()
+    multiply(last)
+    for g in range(last):
+        total = own[g]
+        for k in range(1, ZS):
+            z_copy(g, k).wait_recv()
+            total += z_in[g, k].astype(F32)
+        place_scores(g, total)
+    total = terms[my_terms, :]
+    for i in range(n_peers):
+        term_copy(i).wait_recv()
+        total += last_in[i].astype(F32)
+    place_scores(last, total)
+
+    for g, i in order:
+        send(g, i).wait_send()
     for k in range(1, n_ex):
         query_send(k).wait_send()
+    for g in range(last):
+        x_copy(g).wait_send()
+        for k in range(1, ZS):
+            z_copy(g, k).wait_send()
+    for i in range(n_peers):
+        term_copy(i).wait_send()
+
+
+def in_hbm(array):
+    return pltpu.with_memory_space_constraint(array, pltpu.HBM)
 
 
 def on_device(n_ex, n_mat, train_grads, inverse_hessian, query_grads):
@@ -237,17 +309,18 @@
     all_rows = rows * mats
     group_rows = all_rows // GROUPS
     n_queries = query_grads.shape[0] * n_ex
+    share = n_queries // n_mat
     dma = pltpu.SemaphoreType.DMA
     pre, scores = pl.pallas_call(
         functools.partial(kernel, n_ex, n_mat),
         name="influence",
         out_shape=(
-            jax.ShapeDtypeStruct((all_rows, columns), BF16),
+            pltpu.VMEM((mats, rows, columns), BF16),
             jax.ShapeDtypeStruct((n_queries // n_mat, all_rows), F32),
         ),
         in_specs=[pl.BlockSpec(memory_space=pl.ANY)] * 3,
         out_specs=(
-            pl.BlockSpec(memory_space=pl.ANY),
+            pl.BlockSpec(memory_space=pltpu.VMEM),
             pl.BlockSpec(memory_space=pltpu.VMEM),
         ),
         scratch_shapes=[
@@ -256,9 +329,15 @@
             pltpu.VMEM((GROUPS, group_rows, columns), BF16),
             pltpu.VMEM((columns, columns), BF16),
             pltpu.VMEM((n_queries, columns), BF16),
-            pltpu.VMEM((GROUPS, group_rows, columns), BF16),
-            pltpu.VMEM((GROUPS, n_queries, group_rows), BF16),
-            pltpu.VMEM((GROUPS, n_mat, n_queries // n_mat, group_rows), BF16),
+            pltpu.VMEM((n_queries, columns), BF16),
+            pltpu.VMEM((n_queries, group_rows), F32),
+            pltpu.VMEM((GROUPS - 1, share, group_rows), F32),
+            pltpu.VMEM((GROUPS - 1, n_queries // 2, group_rows), BF16),
+            pltpu.VMEM((GROUPS - 1, n_queries // 2, group_rows), BF16),
+            pltpu.VMEM((GROUPS - 1, n_queries // 2, group_rows), BF16),
+            pltpu.VMEM((GROUPS - 1, ZS, share, group_rows), BF16),
+            pltpu.VMEM((n_queries, group_rows), BF16),
+            pltpu.VMEM((len(PEERS), share, group_rows), BF16),
             dma((GROUPS,)),
             dma,
             dma,
@@ -266,12 +345,15 @@
             dma((GROUPS, n_mat)),
             dma((n_ex,)),
             dma((n_ex,)),
-            dma((GROUPS, n_mat)),
-            dma((GROUPS, n_mat)),
-            dma((GROUPS, n_mat)),
+            dma((GROUPS - 1,)),
+            dma((GROUPS - 1,)),
+            dma((GROUPS - 1, ZS)),
+            dma((GROUPS - 1, ZS)),
+            dma((n_mat,)),
+            dma((n_mat,)),
         ],
         compiler_params=pltpu.CompilerParams(
-            collective_id=0, has_side_effects=True, vmem_limit_bytes=56 * 2**20
+            collective_id=0, has_side_effects=True, vmem_limit_bytes=40 * 2**20
         ),
         cost_estimate=pl.CostEstimate(
             flops=2 * all_rows * columns * (columns + n_queries),
@@ -279,9 +361,9 @@
             transcendentals=0,
         ),
     )(
-        train_grads.reshape(all_rows, columns),
-        inverse_hessian.reshape(columns, columns),
-        query_grads.reshape(query_grads.shape[0], columns),
+        in_hbm(train_grads.reshape(all_rows, columns)),
+        in_hbm(inverse_hessian.reshape(columns, columns)),
+        in_hbm(query_grads.reshape(query_grads.shape[0], columns)),
     )
     return pre.reshape(all_rows, 1, columns), scores
 

time: 125 us -> 120 us (0.960); the launches traced: 125 us -> 118 us
  Pallas kernels: 119 us -> 115 us
  local copies, waits for them, and re-layouts: 5.45 us -> 2.64 us
    pallas_call x1, Pallas kernels: 119 us -> 115 us  [on_device(): pl.pallas_call(functools.partial(kernel, n_ex, n_mat), name='influence',...]
    unnamed x4 -> x2, local copies, waits for them, and re-layouts: 5.45 us -> 2.64 us
where the time goes in v2:
time: 120 us; the launch traced here: 118 us
  Pallas kernels  115 us (96%)
  local copies, waits for them, and re-layouts  2.64 us (2%)
    pallas_call x1, Pallas kernels, on_device(): pl.pallas_call(functools.partial(kernel, n_ex, n_mat), name='influence',...  115 us
    unnamed x2, local copies, waits for them, and re-layouts  2.64 us

profile of v2, /device:TPU:8, one launch (start us, length us, event | category | flops | bytes accessed | tf_op | source)
XLA Modules:
  0.0 118.5 jit_solution(926109065416763549)
XLA Ops:
  0.6 115.2 %influence.1 = (bf16[16,64,2048]{2,1,0:T(8,128)(2,1)S(1)}, f32[16,1024]{1,0:T(8,128)S(1)}) custom-call(bf16[1024,2048]{1,0:T(8,128)(2,1)} %bitcast.6, bf16[2048,2048]{1,0:T(8,128)(2,1)} %bitcast.5, bf16[16,2048]{1,0:T(8,128)(2,1)} %bitcast.7), custom_call_target="tpu_custom_call" | custom-call | flops 9663676416 | bytes 16777216 | tf_op jit(solution)/shard_map/influence/pallas_call | solution.py:314
  115.8 2.0 %copy.7 = bf16[1024,1,2048]{2,0,1:T(8,128)(2,1)} copy(bf16[1024,1,2048]{2,0,1:T(8,128)(2,1)S(1)} %bitcast.4) | data formatting | bytes 8388608
  117.9 0.6 copy.8

commit v3 on v2

--- a/solution.py
+++ b/solution.py
@@ -13,8 +13,7 @@
 ZS = 8
 TILE = 512
 WIDE = 1024
-AHEAD = 8
-PASS_AT = 11
+AHEAD = 22
 
 PEERS = (
     (0, 4), (1, 4), (0, 3), (0, 5), (1, 3), (1, 5), (0, 2), (0, 6),
@@ -80,10 +79,8 @@
     query_load = pltpu.make_async_copy(query_ref, queries.at[my_queries], query_load_sem)
     hess_load = pltpu.make_async_copy(hess_ref, hess, hess_sem)
 
-    for g in range(GROUPS):
-        load(g).start()
+    load(0).start()
     query_load.start()
-    hess_load.start()
 
     barrier = pltpu.get_barrier_semaphore()
     for k in range(1, n_mat):
@@ -241,11 +238,16 @@
     regroup_rows(0)
     query_load.wait()
     pl.semaphore_wait(barrier, n_mat + n_ex - 2)
-    for j in range(AHEAD):
+    for i in range(n_peers):
+        send(0, i).start()
+        query_send(i + 1).start()
+    for g in range(1, GROUPS):
+        load(g).start()
+    hess_load.start()
+    regroup_rows(1)
+    for j in range(n_peers, AHEAD):
         send(*order[j]).start()
-    for k in range(1, n_ex):
-        query_send(k).start()
-    for g in range(1, GROUPS):
+    for g in range(2, GROUPS):
         regroup_rows(g)
     scores_ref[...] = jnp.zeros_like(scores_ref)
     hess_load.wait()
@@ -256,8 +258,6 @@
         arrival(g, i).wait_recv()
         if j + AHEAD < len(order):
             send(*order[j + AHEAD]).start()
-        if i == PASS_AT and g > 0:
-            pass_terms(g - 1)
         if i == 3 and g == 1:
 
             def carry_back(c, carry):
@@ -268,9 +268,12 @@
             lax.fori_loop(0, columns // TILE, carry_back, 0)
         if i == n_peers - 1 and g < GROUPS - 1:
             multiply(g)
+            if g > 0:
+                pass_terms(g - 1)
             start_terms(g)
 
     last = GROUPS - 1
+    pass_terms(last - 1)
     terms[...] = scores_of(carried[...], arrived[last])
     last_out[...] = terms[...].astype(BF16)
     for i in range(n_peers):
@@ -290,8 +293,8 @@
 
     for g, i in order:
         send(g, i).wait_send()
-    for k in range(1, n_ex):
-        query_send(k).wait_send()
+    for i in range(n_peers):
+        query_send(i + 1).wait_send()
     for g in range(last):
         x_copy(g).wait_send()
         for k in range(1, ZS):

time: 120 us -> 117 us (0.975); the launches traced: 118 us -> 117 us
    pallas_call x1, Pallas kernels: 115 us -> 114 us  [on_device(): pl.pallas_call(functools.partial(kernel, n_ex, n_mat), name='influence',...]
where the time goes in v3:
time: 117 us
  Pallas kernels  114 us (97%)
  local copies, waits for them, and re-layouts  2.64 us (2%)
    pallas_call x1, Pallas kernels, on_device(): pl.pallas_call(functools.partial(kernel, n_ex, n_mat), name='influence',...  114 us
    unnamed x2, local copies, waits for them, and re-layouts  2.64 us

profile of v3, /device:TPU:8, one launch (start us, length us, event | category | flops | bytes accessed | tf_op | source)
XLA Modules:
  0.0 116.9 jit_solution(16962734794778178328)
XLA Ops:
  0.6 113.6 %influence.1 = (bf16[16,64,2048]{2,1,0:T(8,128)(2,1)S(1)}, f32[16,1024]{1,0:T(8,128)S(1)}) custom-call(bf16[1024,2048]{1,0:T(8,128)(2,1)} %bitcast.6, bf16[2048,2048]{1,0:T(8,128)(2,1)} %bitcast.5, bf16[16,2048]{1,0:T(8,128)(2,1)} %bitcast.7), custom_call_target="tpu_custom_call" | custom-call | flops 9663676416 | bytes 16777216 | tf_op jit(solution)/shard_map/influence/pallas_call | solution.py:317
  114.3 2.0 %copy.7 = bf16[1024,1,2048]{2,0,1:T(8,128)(2,1)} copy(bf16[1024,1,2048]{2,0,1:T(8,128)(2,1)S(1)} %bitcast.4) | data formatting | bytes 8388608
  116.3 0.6 copy.8

commit v4 on v3

v4 whole, which is shorter than its diff:
```python
import functools

import jax
import jax.numpy as jnp
from jax import lax
from jax.experimental import pallas as pl
from jax.experimental.pallas import tpu as pltpu
from jax.sharding import PartitionSpec as P

MESH = pl.DeviceIdType.MESH
F32, BF16 = jnp.float32, jnp.bfloat16
GROUPS = 4
LAST = GROUPS - 1
ZS = 8
TILE = 512
WIDE = 1024

PEERS = (
    (0, 4), (1, 4), (0, 3), (0, 5), (1, 3), (1, 5), (0, 2), (0, 6),
    (1, 2), (1, 6), (0, 1), (0, 7), (1, 1), (1, 7), (1, 0),
)
Z_PEERS = (4, 3, 5, 2, 6, 1, 7)


def kernel(
    n_ex,
    n_mat,
    train_ref,
    hess_ref,
    query_ref,
    pre_ref,
    own,
    z_in,
    last_in,
    staged,
    outgoing,
    arrived,
    hess,
    queries,
    carried,
    terms,
    x_out,
    x_in,
    z_out,
    last_out,
    load_sem,
    hess_sem,
    query_load_sem,
    send_sem,
    recv_sem,
    query_send_sem,
    query_recv_sem,
    x_send_sem,
    x_recv_sem,
    z_send_sem,
    z_recv_sem,
    term_send_sem,
    term_recv_sem,
):
    me = lax.axis_index("mat")
    my_ex = lax.axis_index("ex")
    side, place = me // ZS, lax.rem(me, ZS)
    z_at = [place] + [lax.rem(place + k, ZS) for k in range(1, ZS)]
    x_at = [side, 1 - side]
    peers = [x_at[dx] * ZS + z_at[dz] for dx, dz in PEERS]
    n_peers = len(PEERS)

    group_rows = train_ref.shape[0] // GROUPS
    part = group_rows // n_mat
    columns = train_ref.shape[1]
    n_queries = queries.shape[0]
    share = n_queries // n_mat
    half = n_queries // 2
    ex_share = query_ref.shape[0]

    mine = pl.ds(pl.multiple_of(me * part, part), part)
    my_queries = pl.ds(pl.multiple_of(my_ex * ex_share, ex_share), ex_share)
    my_half = pl.ds(pl.multiple_of(side * half, half), half)
    other_half = pl.ds(pl.multiple_of((1 - side) * half, half), half)
    my_terms = pl.ds(pl.multiple_of(me * share, share), share)

    def load(g):
        rows = pl.ds(g * group_rows, group_rows)
        return pltpu.make_async_copy(train_ref.at[rows], staged.at[g], load_sem.at[g])

    query_load = pltpu.make_async_copy(query_ref, queries.at[my_queries], query_load_sem)
    hess_load = pltpu.make_async_copy(hess_ref, hess, hess_sem)

    load(0).start()
    query_load.start()
    barrier = pltpu.get_barrier_semaphore()
    for to in peers:
        pl.semaphore_signal(barrier, inc=1, device_id={"mat": to}, device_id_type=MESH)
    ex_peers = [lax.rem(my_ex + k, n_ex) for k in range(1, n_ex)]
    for to in ex_peers:
        pl.semaphore_signal(barrier, inc=1, device_id={"ex": to}, device_id_type=MESH)

    out_row = lax.broadcasted_iota(jnp.int32, (group_rows, group_rows), 0)
    in_row = lax.broadcasted_iota(jnp.int32, (group_rows, group_rows), 1)
    regroup = jnp.where(
        in_row == lax.rem(out_row, part) * n_mat + out_row // part, 1.0, 0.0
    ).astype(BF16)

    def regroup_rows(g):
        load(g).wait()
        for c in range(columns // TILE):
            cols = pl.ds(c * TILE, TILE)
            outgoing[g, :, cols] = jnp.dot(
                regroup, staged[g, :, cols], preferred_element_type=F32
            ).astype(BF16)
        arrived[g, mine, :] = outgoing[g, mine, :]

    def to_mat(src, dst, sent, received, device):
        return pltpu.make_async_remote_copy(
            src_ref=src,
            dst_ref=dst,
            send_sem=sent,
            recv_sem=received,
            device_id={"mat": device},
            device_id_type=MESH,
        )

    def send(g, i):
        rows = pl.ds(pl.multiple_of(peers[i] * part, part), part)
        return to_mat(
            outgoing.at[g, rows], arrived.at[g, mine], send_sem.at[g], recv_sem.at[g], peers[i]
        )

    def all_sends(g):
        rows = pl.ds(0, part * n_peers)
        return to_mat(
            outgoing.at[g, rows], arrived.at[g, rows], send_sem.at[g], recv_sem.at[g], peers[0]
        )

    def to_ex(rows, device):
        return pltpu.make_async_remote_copy(
            src_ref=queries.at[rows],
            dst_ref=queries.at[rows],
            send_sem=query_send_sem,
            recv_sem=query_recv_sem,
            device_id={"ex": device},
            device_id_type=MESH,
        )

    all_query_sends = to_ex(pl.ds(0, ex_share * (n_ex - 1)), ex_peers[0])

    def x_copy(g):
        return to_mat(x_out.at[g], x_in.at[g], x_send_sem.at[g], x_recv_sem.at[g], peers[-1])

    def z_copy(g, i):
        to = z_at[Z_PEERS[i]]
        return to_mat(
            z_out.at[g, pl.ds(pl.multiple_of(to * share, share), share)],
            z_in.at[g, i],
            z_send_sem.at[g],
            z_recv_sem.at[g],
            side * ZS + to,
        )

    def all_z(g):
        slots = pl.ds(0, len(Z_PEERS))
        return to_mat(
            z_in.at[g, slots], z_in.at[g, slots], z_send_sem.at[g], z_recv_sem.at[g], peers[0]
        )

    def term_copy(i):
        rows = pl.ds(pl.multiple_of(peers[i] * share, share), share)
        return to_mat(last_out.at[rows], last_in.at[i], term_send_sem, term_recv_sem, peers[i])

    all_terms = to_mat(last_in, last_in, term_send_sem, term_recv_sem, peers[0])

    def multiply(g):
        def tile(c, carry):
            cols = pl.ds(pl.multiple_of(c * WIDE, WIDE), WIDE)
            product = jnp.dot(arrived[g], hess[:, cols], preferred_element_type=F32)
            pre_ref[:, pl.ds(g * part, part), cols] = product.astype(BF16).reshape(
                n_mat, part, WIDE
            )
            return carry

        lax.fori_loop(0, columns // WIDE, tile, 0)

    def scores_of(left, rows):
        return lax.dot_general(left, rows, (((1,), (1,)), ((), ())), preferred_element_type=F32)

    def start_terms(g):
        rows = pre_ref[:, pl.ds(g * part, part), :].reshape(group_rows, columns)
        terms[...] = scores_of(queries[...], rows)
        x_out[g] = terms[other_half, :].astype(BF16)
        x_copy(g).start()

    def pass_terms(g):
        x_copy(g).wait_recv()
        terms[my_half, :] = terms[my_half, :] + x_in[g].astype(F32)
        z_out[g] = terms[my_half, :].astype(BF16)
        for i in range(len(Z_PEERS)):
            z_copy(g, i).start()
        own[g] = terms[my_terms, :]

    regroup_rows(0)
    query_load.wait()
    pl.semaphore_wait(barrier, n_mat + n_ex - 2)
    for i in range(n_peers):
        send(0, i).start()
        to_ex(my_queries, ex_peers[i]).start()
    for g in range(1, GROUPS):
        load(g).start()
    hess_load.start()
    regroup_rows(1)
    for i in range(n_peers):
        send(1, i).start()
    for g in range(2, GROUPS):
        regroup_rows(g)
    hess_load.wait()
    all_query_sends.wait_recv()

    for g in range(GROUPS):
        all_sends(g).wait_recv()
        if g + 2 < GROUPS:
            for i in range(n_peers):
                send(g + 2, i).start()
        if g < LAST:
            multiply(g)
            if g > 0:
                pass_terms(g - 1)
            start_terms(g)
        if g == 0:
            all_query_sends.wait_send()

            def carry_back(c, carry):
                cols = pl.ds(pl.multiple_of(c * TILE, TILE), TILE)
                carried[:, cols] = scores_of(queries[...], hess[cols, :]).astype(BF16)
                return carry

            lax.fori_loop(0, columns // TILE, carry_back, 0)
        else:
            all_sends(g - 1).wait_send()

    pass_terms(LAST - 1)
    terms[...] = scores_of(carried[...], arrived[LAST])
    last_out[...] = terms[...].astype(BF16)
    for i in range(n_peers):
        term_copy(i).start()
    own[LAST] = terms[my_terms, :]
    multiply(LAST)

    all_sends(LAST).wait_send()
    for g in range(LAST):
        x_copy(g).wait_send()
        all_z(g).wait_send()
        all_z(g).wait_recv()
    all_terms.wait_send()
    all_terms.wait_recv()


def finish(pre_ref, own, z_in, last_in, out_ref, scores_ref, scores, out_sem, scores_sem):
    n_mat = pre_ref.shape[0]
    pieces = out_sem.shape[0]
    step = n_mat // pieces
    part = own.shape[2] // n_mat

    def out_copy(k):
        mats = pl.ds(k * step, step)
        return pltpu.make_async_copy(pre_ref.at[mats], out_ref.at[mats], out_sem.at[k])

    for k in range(pieces):
        out_copy(k).start()
    totals = []
    for g in range(GROUPS):
        total = own[g]
        if g < LAST:
            for i in range(len(Z_PEERS)):
                total += z_in[g, i].astype(F32)
        else:
            for i in range(len(PEERS)):
                total += last_in[i].astype(F32)
        totals.append(total)
    lane = lax.broadcasted_iota(jnp.int32, (own.shape[1], 128), 1)
    for j in range(scores.shape[1] // 128):
        tile = jnp.zeros(lane.shape, F32)
        for s in range(2):
            at, of = ((2 * j + s) * part) % 128, (2 * j + s) * part // 128
            for g in range(GROUPS):
                to = (s * GROUPS + g) * part
                moved = pltpu.roll(totals[g][:, of * 128 : of * 128 + 128], (to - at) % 128, 1)
                tile = jnp.where((lane >= to) & (lane < to + part), moved, tile)
        scores[:, j * 128 : j * 128 + 128] = tile
    scores_copy = pltpu.make_async_copy(scores, scores_ref, scores_sem)
    scores_copy.start()
    for k in range(pieces):
        out_copy(k).wait()
    scores_copy.wait()


def in_hbm(array):
    return pltpu.with_memory_space_constraint(array, pltpu.HBM)


def on_device(n_ex, n_mat, train_grads, inverse_hessian, query_grads):
    rows, mats, columns = train_grads.shape
    all_rows = rows * mats
    group_rows = all_rows // GROUPS
    n_queries = query_grads.shape[0] * n_ex
    share = n_queries // n_mat
    dma = pltpu.SemaphoreType.DMA
    in_vmem = pl.BlockSpec(memory_space=pltpu.VMEM)
    anywhere = pl.BlockSpec(memory_space=pl.ANY)
    parts = pl.pallas_call(
        functools.partial(kernel, n_ex, n_mat),
        name="influence",
        out_shape=(
            pltpu.VMEM((mats, rows, columns), BF16),
            pltpu.VMEM((GROUPS, share, group_rows), F32),
            pltpu.VMEM((LAST, len(Z_PEERS), share, group_rows), BF16),
            pltpu.VMEM((len(PEERS), share, group_rows), BF16),
        ),
        in_specs=[anywhere] * 3,
        out_specs=(in_vmem,) * 4,
        scratch_shapes=[
            pltpu.VMEM((GROUPS, group_rows, columns), BF16),
            pltpu.VMEM((GROUPS, group_rows, columns), BF16),
            pltpu.VMEM((GROUPS, group_rows, columns), BF16),
            pltpu.VMEM((columns, columns), BF16),
            pltpu.VMEM((n_queries, columns), BF16),
            pltpu.VMEM((n_queries, columns), BF16),
            pltpu.VMEM((n_queries, group_rows), F32),
            pltpu.VMEM((LAST, n_queries // 2, group_rows), BF16),
            pltpu.VMEM((LAST, n_queries // 2, group_rows), BF16),
            pltpu.VMEM((LAST, n_queries // 2, group_rows), BF16),
            pltpu.VMEM((n_queries, group_rows), BF16),
            dma((GROUPS,)),
            dma,
            dma,
            dma((GROUPS,)),
            dma((GROUPS,)),
            dma,
            dma,
            dma((LAST,)),
            dma((LAST,)),
            dma((LAST,)),
            dma((LAST,)),
            dma,
            dma,
        ],
        compiler_params=pltpu.CompilerParams(
            collective_id=0, has_side_effects=True, vmem_limit_bytes=40 * 2**20
        ),
        cost_estimate=pl.CostEstimate(
            flops=2 * all_rows * columns * (columns + n_queries),
            bytes_accessed=2 * columns * (2 * all_rows + columns),
            transcendentals=0,
        ),
    )(
        in_hbm(train_grads.reshape(all_rows, columns)),
        in_hbm(inverse_hessian.reshape(columns, columns)),
        in_hbm(query_grads.reshape(query_grads.shape[0], columns)),
    )
    pre, scores = pl.pallas_call(
        finish,
        name="write_out",
        out_shape=(
            pltpu.HBM((mats, rows, columns), BF16),
            pltpu.HBM((share, all_rows), F32),
        ),
        in_specs=[in_vmem] * 4,
        out_specs=(anywhere,) * 2,
        scratch_shapes=[pltpu.VMEM((share, all_rows), F32), dma((4,)), dma],
        compiler_params=pltpu.CompilerParams(vmem_limit_bytes=16 * 2**20),
    )(*parts)
    return pre.reshape(all_rows, 1, columns), scores


def solution(mesh):
    return jax.shard_map(
        functools.partial(on_device, mesh.shape["ex"], mesh.shape["mat"]),
        mesh=mesh,
        in_specs=(P(("ex", "mat"), None, None), P("mat", None, None), P("ex", "mat", None)),
        out_specs=(P("ex", "mat", None), P("mat", "ex")),
        check_vma=False,
    )
```

time: 117 us -> 113 us (0.966)
  local copies, waits for them, and re-layouts: 2.64 us -> 0 us
  Pallas kernels: 114 us -> 112 us
    pallas_call x1, Pallas kernels: 114 us -> 110 us  [on_device(): pl.pallas_call(functools.partial(kernel, n_ex, n_mat), name='influence',...]
    unnamed x2 -> x0, local copies, waits for them, and re-layouts: 2.64 us -> none
    pallas_call x0 -> x1, Pallas kernels: none -> 2.18 us  [on_device(): pl.pallas_call(finish, name='write_out', out_shape=(pltpu.HBM((mats, rows...]
where the time goes in v4:
time: 113 us
  Pallas kernels  112 us (99%)
    pallas_call x1, Pallas kernels, on_device(): pl.pallas_call(functools.partial(kernel, n_ex, n_mat), name='influence',...  110 us

profile of v4, /device:TPU:8, one launch (start us, length us, event | category | flops | bytes accessed | tf_op | source)
XLA Modules:
  0.0 112.9 jit_solution(15190024619531196166)
XLA Ops:
  0.6 110.0 %influence.1 = (bf16[16,64,2048]{2,1,0:T(8,128)(2,1)S(1)}, f32[4,16,256]{2,1,0:T(8,128)S(1)}, bf16[3,7,16,256]{3,2,1,0:T(8,128)(2,1)S(1)}, bf16[15,16,256]{2,1,0:T(8,128)(2,1)S(1)}) custom-call(bf16[1024,2048]{1,0:T(8,128)(2,1)} %bitcast.5, bf16[2048,2048]{1,0:T(8,128)(2,1)} %bitcast.4, bf16[16,2048]{1,0:T(8,128)(2,1)} %bitcast.7), custom_call_target="tpu_custom_call" | custom-call | flops 9663676416 | bytes 16777216 | tf_op jit(solution)/shard_map/influence/pallas_call | solution.py:308
  110.7 2.2 %write_out.1 = (bf16[16,64,2048]{2,1,0:T(8,128)(2,1)}, f32[16,1024]{1,0:T(8,128)}) custom-call(bf16[16,64,2048]{2,1,0:T(8,128)(2,1)S(1)} %get-tuple-element.8.pre_ref, f32[4,16,256]{2,1,0:T(8,128)S(1)} %get-tuple-element.9.own, bf16[3,7,16,256]{3,2,1,0:T(8,128)(2,1)S(1)} %get-tuple-element.10.z_in, bf16[15,16,256]{2,1,0:T(8,128)(2,1)S(1)} %get-tuple-element.11.last_in), custom_call_target="tpu_custom_call" | custom-call | tf_op jit(solution)/shard_map/write_out/pallas_call | solution.py:358

commit v5 on v4

--- a/solution.py
+++ b/solution.py
@@ -20,6 +20,8 @@
     (1, 2), (1, 6), (0, 1), (0, 7), (1, 1), (1, 7), (1, 0),
 )
 Z_PEERS = (4, 3, 5, 2, 6, 1, 7)
+SAME = tuple(i for i, (dx, dz) in enumerate(PEERS) if dz % 2 == 0)
+OTHER = tuple(i for i, (dx, dz) in enumerate(PEERS) if dz % 2 == 1)
 
 
 def kernel(
@@ -30,6 +32,7 @@
     query_ref,
     pre_ref,
     own,
+    own_last,
     z_in,
     last_in,
     staged,
@@ -43,6 +46,7 @@
     x_in,
     z_out,
     last_out,
+    last_terms_out,
     load_sem,
     hess_sem,
     query_load_sem,
@@ -73,7 +77,10 @@
     half = n_queries // 2
     ex_share = query_ref.shape[0]
 
+    parity = lax.rem(place, 2)
     mine = pl.ds(pl.multiple_of(me * part, part), part)
+    slot = parity * (n_mat // 2) + side * (ZS // 2) + place // 2
+    my_slot = pl.ds(pl.multiple_of(slot * part, part), part)
     my_queries = pl.ds(pl.multiple_of(my_ex * ex_share, ex_share), ex_share)
     my_half = pl.ds(pl.multiple_of(side * half, half), half)
     other_half = pl.ds(pl.multiple_of((1 - side) * half, half), half)
@@ -108,7 +115,7 @@
             outgoing[g, :, cols] = jnp.dot(
                 regroup, staged[g, :, cols], preferred_element_type=F32
             ).astype(BF16)
-        arrived[g, mine, :] = outgoing[g, mine, :]
+        arrived[g, my_slot, :] = outgoing[g, mine, :]
 
     def to_mat(src, dst, sent, received, device):
         return pltpu.make_async_remote_copy(
@@ -122,14 +129,17 @@
 
     def send(g, i):
         rows = pl.ds(pl.multiple_of(peers[i] * part, part), part)
+        k = g + 1 if g == LAST and i in OTHER else g
         return to_mat(
-            outgoing.at[g, rows], arrived.at[g, mine], send_sem.at[g], recv_sem.at[g], peers[i]
-        )
-
-    def all_sends(g):
-        rows = pl.ds(0, part * n_peers)
+            outgoing.at[g, rows], arrived.at[g, my_slot], send_sem.at[k], recv_sem.at[k], peers[i]
+        )
+
+    def all_sends(k):
+        count = n_peers if k < LAST else len(SAME) if k == LAST else len(OTHER)
+        rows = pl.ds(0, part * count)
+        g = min(k, LAST)
         return to_mat(
-            outgoing.at[g, rows], arrived.at[g, rows], send_sem.at[g], recv_sem.at[g], peers[0]
+            outgoing.at[g, rows], arrived.at[g, rows], send_sem.at[k], recv_sem.at[k], peers[0]
         )
 
     def to_ex(rows, device):
@@ -163,9 +173,12 @@
             z_in.at[g, slots], z_in.at[g, slots], z_send_sem.at[g], z_recv_sem.at[g], peers[0]
         )
 
-    def term_copy(i):
+    def term_copy(h, i):
         rows = pl.ds(pl.multiple_of(peers[i] * share, share), share)
-        return to_mat(last_out.at[rows], last_in.at[i], term_send_sem, term_recv_sem, peers[i])
+        to = parity if h == 0 else 1 - parity
+        return to_mat(
+            last_out.at[h, rows], last_in.at[i, to], term_send_sem, term_recv_sem, peers[i]
+        )
 
     all_terms = to_mat(last_in, last_in, term_send_sem, term_recv_sem, peers[0])
 
@@ -173,9 +186,10 @@
         def tile(c, carry):
             cols = pl.ds(pl.multiple_of(c * WIDE, WIDE), WIDE)
             product = jnp.dot(arrived[g], hess[:, cols], preferred_element_type=F32)
-            pre_ref[:, pl.ds(g * part, part), cols] = product.astype(BF16).reshape(
-                n_mat, part, WIDE
-            )
+            product = product.astype(BF16).reshape(n_mat, part, WIDE)
+            for at in range(n_mat):
+                odd, x, z = at // (n_mat // 2), at // (ZS // 2) % 2, at % (ZS // 2)
+                pre_ref[x * ZS + 2 * z + odd, pl.ds(g * part, part), cols] = product[at]
             return carry
 
         lax.fori_loop(0, columns // WIDE, tile, 0)
@@ -214,16 +228,24 @@
     hess_load.wait()
     all_query_sends.wait_recv()
 
-    for g in range(GROUPS):
+    def last_terms(h):
+        at = parity if h == 0 else 1 - parity
+        rows = pl.ds(pl.multiple_of(at * (group_rows // 2), group_rows // 2), group_rows // 2)
+        product = scores_of(carried[...], arrived[LAST, rows, :])
+        last_terms_out[...] = product
+        last_out[h] = product.astype(BF16)
+        for i in range(n_peers):
+            term_copy(h, i).start()
+        own_last[at] = last_terms_out[my_terms, :]
+
+    for g in range(LAST):
         all_sends(g).wait_recv()
-        if g + 2 < GROUPS:
-            for i in range(n_peers):
-                send(g + 2, i).start()
-        if g < LAST:
-            multiply(g)
-            if g > 0:
-                pass_terms(g - 1)
-            start_terms(g)
+        multiply(g)
+        if g > 0:
+            pass_terms(g - 1)
+        start_terms(g)
+        for i in range(n_peers) if g == 0 else SAME if g == 1 else OTHER:
+            send(min(g + 2, LAST), i).start()
         if g == 0:
             all_query_sends.wait_send()
 
@@ -236,15 +258,15 @@
         else:
             all_sends(g - 1).wait_send()
 
+    all_sends(LAST).wait_recv()
+    last_terms(0)
     pass_terms(LAST - 1)
-    terms[...] = scores_of(carried[...], arrived[LAST])
-    last_out[...] = terms[...].astype(BF16)
-    for i in range(n_peers):
-        term_copy(i).start()
-    own[LAST] = terms[my_terms, :]
+    all_sends(LAST + 1).wait_recv()
+    last_terms(1)
     multiply(LAST)
 
-    all_sends(LAST).wait_send()
+    for k in range(LAST - 1, LAST + 2):
+        all_sends(k).wait_send()
     for g in range(LAST):
         x_copy(g).wait_send()
         all_z(g).wait_send()
@@ -253,7 +275,7 @@
     all_terms.wait_recv()
 
 
-def finish(pre_ref, own, z_in, last_in, out_ref, scores_ref, scores, out_sem, scores_sem):
+def finish(pre_ref, own, own_last, z_in, last_in, out_ref, scores_ref, scores, out_sem, scores_sem):
     n_mat = pre_ref.shape[0]
     pieces = out_sem.shape[0]
     step = n_mat // pieces
@@ -266,23 +288,27 @@
     for k in range(pieces):
         out_copy(k).start()
     totals = []
-    for g in range(GROUPS):
+    for g in range(LAST):
         total = own[g]
-        if g < LAST:
-            for i in range(len(Z_PEERS)):
-                total += z_in[g, i].astype(F32)
-        else:
-            for i in range(len(PEERS)):
-                total += last_in[i].astype(F32)
+        for i in range(len(Z_PEERS)):
+            total += z_in[g, i].astype(F32)
+        totals += [total[:, :128], total[:, 128:]]
+    for h in range(2):
+        total = own_last[h]
+        for i in range(len(PEERS)):
+            total += last_in[i, h].astype(F32)
         totals.append(total)
     lane = lax.broadcasted_iota(jnp.int32, (own.shape[1], 128), 1)
-    for j in range(scores.shape[1] // 128):
+    for j in range(n_mat // 2):
         tile = jnp.zeros(lane.shape, F32)
         for s in range(2):
-            at, of = ((2 * j + s) * part) % 128, (2 * j + s) * part // 128
+            mat = 2 * j + s
             for g in range(GROUPS):
+                x, z = mat // ZS, mat % ZS
+                slot = mat if g < LAST else z % 2 * (n_mat // 2) + x * (ZS // 2) + z // 2
+                at, half = (slot * part) % 128, slot * part // 128
                 to = (s * GROUPS + g) * part
-                moved = pltpu.roll(totals[g][:, of * 128 : of * 128 + 128], (to - at) % 128, 1)
+                moved = pltpu.roll(totals[2 * g + half], (to - at) % 128, 1)
                 tile = jnp.where((lane >= to) & (lane < to + part), moved, tile)
         scores[:, j * 128 : j * 128 + 128] = tile
     scores_copy = pltpu.make_async_copy(scores, scores_ref, scores_sem)
@@ -310,12 +336,13 @@
         name="influence",
         out_shape=(
             pltpu.VMEM((mats, rows, columns), BF16),
-            pltpu.VMEM((GROUPS, share, group_rows), F32),
+            pltpu.VMEM((LAST, share, group_rows), F32),
+            pltpu.VMEM((2, share, group_rows // 2), F32),
             pltpu.VMEM((LAST, len(Z_PEERS), share, group_rows), BF16),
-            pltpu.VMEM((len(PEERS), share, group_rows), BF16),
+            pltpu.VMEM((len(PEERS), 2, share, group_rows // 2), BF16),
         ),
         in_specs=[anywhere] * 3,
-        out_specs=(in_vmem,) * 4,
+        out_specs=(in_vmem,) * 5,
         scratch_shapes=[
             pltpu.VMEM((GROUPS, group_rows, columns), BF16),
             pltpu.VMEM((GROUPS, group_rows, columns), BF16),
@@ -327,12 +354,13 @@
             pltpu.VMEM((LAST, n_queries // 2, group_rows), BF16),
             pltpu.VMEM((LAST, n_queries // 2, group_rows), BF16),
             pltpu.VMEM((LAST, n_queries // 2, group_rows), BF16),
-            pltpu.VMEM((n_queries, group_rows), BF16),
+            pltpu.VMEM((2, n_queries, group_rows // 2), BF16),
+            pltpu.VMEM((n_queries, group_rows // 2), F32),
             dma((GROUPS,)),
             dma,
             dma,
-            dma((GROUPS,)),
-            dma((GROUPS,)),
+            dma((GROUPS + 1,)),
+            dma((GROUPS + 1,)),
             dma,
             dma,
             dma((LAST,)),
@@ -362,7 +390,7 @@
             pltpu.HBM((mats, rows, columns), BF16),
             pltpu.HBM((share, all_rows), F32),
         ),
-        in_specs=[in_vmem] * 4,
+        in_specs=[in_vmem] * 5,
         out_specs=(anywhere,) * 2,
         scratch_shapes=[pltpu.VMEM((share, all_rows), F32), dma((4,)), dma],
         compiler_params=pltpu.CompilerParams(vmem_limit_bytes=16 * 2**20),

time: 113 us -> 115 us (1.018)
  Pallas kernels: 112 us -> 114 us
    pallas_call x1, Pallas kernels: 110 us -> 111 us  [on_device(): pl.pallas_call(functools.partial(kernel, n_ex, n_mat), name='influence',...]
where the time goes in v5:
time: 115 us; the launch traced here: 114 us
  Pallas kernels  114 us (99%)
    pallas_call x1, Pallas kernels, on_device(): pl.pallas_call(functools.partial(kernel, n_ex, n_mat), name='influence',...  111 us

profile of v5, /device:TPU:8, one launch (start us, length us, event | category | flops | bytes accessed | tf_op | source)
XLA Modules:
  0.0 114.3 jit_solution(7993909368084270430)
XLA Ops:
  0.6 111.5 %influence.1 = (bf16[16,64,2048]{2,1,0:T(8,128)(2,1)S(1)}, f32[3,16,256]{2,1,0:T(8,128)S(1)}, f32[2,16,128]{2,1,0:T(8,128)S(1)}, bf16[3,7,16,256]{3,2,1,0:T(8,128)(2,1)S(1)}, bf16[15,2,16,128]{3,2,1,0:T(8,128)(2,1)S(1)}) custom-call(bf16[1024,2048]{1,0:T(8,128)(2,1)} %bitcast.5, bf16[2048,2048]{1,0:T(8,128)(2,1)} %bitcast.4, bf16[16,2048]{1,0:T(8,128)(2,1)} %bitcast.7), custom_call_target="tpu_custom_call" | custom-call | flops 9663676416 | bytes 16777216 | tf_op jit(solution)/shard_map/influence/pallas_call | solution.py:334
  112.1 2.2 %write_out.1 = (bf16[16,64,2048]{2,1,0:T(8,128)(2,1)}, f32[16,1024]{1,0:T(8,128)}) custom-call(bf16[16,64,2048]{2,1,0:T(8,128)(2,1)S(1)} %get-tuple-element.9.pre_ref, f32[3,16,256]{2,1,0:T(8,128)S(1)} %get-tuple-element.10.own, f32[2,16,128]{2,1,0:T(8,128)S(1)} %get-tuple-element.11.own_last, bf16[3,7,16,256]{3,2,1,0:T(8,128)(2,1)S(1)} %get-tuple-element.12.z_in, ...), custom_call_target="tpu_custom_call" | custom-call | tf_op jit(solution)/shard_map/write_out/pallas_call | solution.py:386

commit v6 on v5

--- a/solution.py
+++ b/solution.py
@@ -93,12 +93,16 @@
     query_load = pltpu.make_async_copy(query_ref, queries.at[my_queries], query_load_sem)
     hess_load = pltpu.make_async_copy(hess_ref, hess, hess_sem)
 
-    load(0).start()
+    quarter = group_rows // 4
+    for k in range(4):
+        rows = pl.ds(k * quarter, quarter)
+        pltpu.make_async_copy(train_ref.at[rows], staged.at[0, rows], load_sem.at[0]).start()
     query_load.start()
     barrier = pltpu.get_barrier_semaphore()
     for to in peers:
         pl.semaphore_signal(barrier, inc=1, device_id={"mat": to}, device_id_type=MESH)
-    ex_peers = [lax.rem(my_ex + k, n_ex) for k in range(1, n_ex)]
+    core = lax.rem(my_ex, 2)
+    ex_peers = [my_ex + 1 - 2 * core] + [lax.rem(my_ex + k, n_ex) for k in range(2, n_ex, 2)]
     for to in ex_peers:
         pl.semaphore_signal(barrier, inc=1, device_id={"ex": to}, device_id_type=MESH)
 
@@ -142,17 +146,20 @@
             outgoing.at[g, rows], arrived.at[g, rows], send_sem.at[k], recv_sem.at[k], peers[0]
         )
 
-    def to_ex(rows, device):
+    def to_ex(rows, sem, device):
         return pltpu.make_async_remote_copy(
             src_ref=queries.at[rows],
             dst_ref=queries.at[rows],
-            send_sem=query_send_sem,
-            recv_sem=query_recv_sem,
+            send_sem=query_send_sem.at[sem],
+            recv_sem=query_recv_sem.at[sem],
             device_id={"ex": device},
             device_id_type=MESH,
         )
 
-    all_query_sends = to_ex(pl.ds(0, ex_share * (n_ex - 1)), ex_peers[0])
+    pair_rows = 2 * ex_share
+    my_pair = pl.ds(pl.multiple_of(my_ex // 2 * pair_rows, pair_rows), pair_rows)
+    to_core = to_ex(my_queries, 0, ex_peers[0])
+    all_pairs = to_ex(pl.ds(0, pair_rows * (len(ex_peers) - 1)), 1, ex_peers[1])
 
     def x_copy(g):
         return to_mat(x_out.at[g], x_in.at[g], x_send_sem.at[g], x_recv_sem.at[g], peers[-1])
@@ -213,20 +220,21 @@
 
     regroup_rows(0)
     query_load.wait()
-    pl.semaphore_wait(barrier, n_mat + n_ex - 2)
+    pl.semaphore_wait(barrier, len(peers) + len(ex_peers))
+    to_core.start()
     for i in range(n_peers):
         send(0, i).start()
-        to_ex(my_queries, ex_peers[i]).start()
     for g in range(1, GROUPS):
         load(g).start()
     hess_load.start()
+    to_core.wait_recv()
+    for to in ex_peers[1:]:
+        to_ex(my_pair, 1, to).start()
     regroup_rows(1)
     for i in range(n_peers):
         send(1, i).start()
     for g in range(2, GROUPS):
         regroup_rows(g)
-    hess_load.wait()
-    all_query_sends.wait_recv()
 
     def last_terms(h):
         at = parity if h == 0 else 1 - parity
@@ -240,14 +248,16 @@
 
     for g in range(LAST):
         all_sends(g).wait_recv()
+        for i in range(n_peers) if g + 2 <= LAST else ():
+            send(g + 2, i).start()
+        if g == 0:
+            all_pairs.wait_recv()
+            hess_load.wait()
         multiply(g)
         if g > 0:
             pass_terms(g - 1)
         start_terms(g)
-        for i in range(n_peers) if g == 0 else SAME if g == 1 else OTHER:
-            send(min(g + 2, LAST), i).start()
         if g == 0:
-            all_query_sends.wait_send()
 
             def carry_back(c, carry):
                 cols = pl.ds(pl.multiple_of(c * TILE, TILE), TILE)
@@ -265,6 +275,8 @@
     last_terms(1)
     multiply(LAST)
 
+    to_core.wait_send()
+    all_pairs.wait_send()
     for k in range(LAST - 1, LAST + 2):
         all_sends(k).wait_send()
     for g in range(LAST):
@@ -361,8 +373,8 @@
             dma,
             dma((GROUPS + 1,)),
             dma((GROUPS + 1,)),
-            dma,
-            dma,
+            dma((2,)),
+            dma((2,)),
             dma((LAST,)),
             dma((LAST,)),
             dma((LAST,)),

time: 115 us -> 113 us (0.983)
  Pallas kernels: 114 us -> 111 us
    pallas_call x1, Pallas kernels: 111 us -> 109 us  [on_device(): pl.pallas_call(functools.partial(kernel, n_ex, n_mat), name='influence',...]
where the time goes in v6:
time: 113 us; the launch traced here: 112 us
  Pallas kernels  111 us (98%)
    pallas_call x1, Pallas kernels, on_device(): pl.pallas_call(functools.partial(kernel, n_ex, n_mat), name='influence',...  109 us

profile of v6, /device:TPU:8, one launch (start us, length us, event | category | flops | bytes accessed | tf_op | source)
XLA Modules:
  0.0 112.1 jit_solution(16653320944832465697)
XLA Ops:
  0.6 109.2 %influence.1 = (bf16[16,64,2048]{2,1,0:T(8,128)(2,1)S(1)}, f32[3,16,256]{2,1,0:T(8,128)S(1)}, f32[2,16,128]{2,1,0:T(8,128)S(1)}, bf16[3,7,16,256]{3,2,1,0:T(8,128)(2,1)S(1)}, bf16[15,2,16,128]{3,2,1,0:T(8,128)(2,1)S(1)}) custom-call(bf16[1024,2048]{1,0:T(8,128)(2,1)} %bitcast.5, bf16[2048,2048]{1,0:T(8,128)(2,1)} %bitcast.4, bf16[16,2048]{1,0:T(8,128)(2,1)} %bitcast.7), custom_call_target="tpu_custom_call" | custom-call | flops 9663676416 | bytes 16777216 | tf_op jit(solution)/shard_map/influence/pallas_call | solution.py:346
  109.9 2.2 %write_out.1 = (bf16[16,64,2048]{2,1,0:T(8,128)(2,1)}, f32[16,1024]{1,0:T(8,128)}) custom-call(bf16[16,64,2048]{2,1,0:T(8,128)(2,1)S(1)} %get-tuple-element.9.pre_ref, f32[3,16,256]{2,1,0:T(8,128)S(1)} %get-tuple-element.10.own, f32[2,16,128]{2,1,0:T(8,128)S(1)} %get-tuple-element.11.own_last, bf16[3,7,16,256]{3,2,1,0:T(8,128)(2,1)S(1)} %get-tuple-element.12.z_in, ...), custom_call_target="tpu_custom_call" | custom-call | tf_op jit(solution)/shard_map/write_out/pallas_call | solution.py:398

commit v7 on v6

--- a/solution.py
+++ b/solution.py
@@ -13,7 +13,7 @@
 LAST = GROUPS - 1
 ZS = 8
 TILE = 512
-WIDE = 1024
+WIDE = 2048
 
 PEERS = (
     (0, 4), (1, 4), (0, 3), (0, 5), (1, 3), (1, 5), (0, 2), (0, 6),
@@ -270,9 +270,9 @@
 
     all_sends(LAST).wait_recv()
     last_terms(0)
-    pass_terms(LAST - 1)
     all_sends(LAST + 1).wait_recv()
     last_terms(1)
+    pass_terms(LAST - 1)
     multiply(LAST)
 
     to_core.wait_send()

time: 113 us -> 113 us (level)
  no operation moved by 1% of the time
where the time goes in v7:
time: 113 us; the launch traced here: 112 us
  Pallas kernels  111 us (98%)
    pallas_call x1, Pallas kernels, on_device(): pl.pallas_call(functools.partial(kernel, n_ex, n_mat), name='influence',...  109 us

profile of v7, /device:TPU:8, one launch (start us, length us, event | category | flops | bytes accessed | tf_op | source)
XLA Modules:
  0.0 111.7 jit_solution(11440965726972045053)
XLA Ops:
  0.6 108.9 %influence.1 = (bf16[16,64,2048]{2,1,0:T(8,128)(2,1)S(1)}, f32[3,16,256]{2,1,0:T(8,128)S(1)}, f32[2,16,128]{2,1,0:T(8,128)S(1)}, bf16[3,7,16,256]{3,2,1,0:T(8,128)(2,1)S(1)}, bf16[15,2,16,128]{3,2,1,0:T(8,128)(2,1)S(1)}) custom-call(bf16[1024,2048]{1,0:T(8,128)(2,1)} %bitcast.5, bf16[2048,2048]{1,0:T(8,128)(2,1)} %bitcast.4, bf16[16,2048]{1,0:T(8,128)(2,1)} %bitcast.7), custom_call_target="tpu_custom_call" | custom-call | flops 9663676416 | bytes 16777216 | tf_op jit(solution)/shard_map/influence/pallas_call | solution.py:346
  109.6 2.2 %write_out.1 = (bf16[16,64,2048]{2,1,0:T(8,128)(2,1)}, f32[16,1024]{1,0:T(8,128)}) custom-call(bf16[16,64,2048]{2,1,0:T(8,128)(2,1)S(1)} %get-tuple-element.9.pre_ref, f32[3,16,256]{2,1,0:T(8,128)S(1)} %get-tuple-element.10.own, f32[2,16,128]{2,1,0:T(8,128)S(1)} %get-tuple-element.11.own_last, bf16[3,7,16,256]{3,2,1,0:T(8,128)(2,1)S(1)} %get-tuple-element.12.z_in, ...), custom_call_target="tpu_custom_call" | custom-call | tf_op jit(solution)/shard_map/write_out/pallas_call | solution.py:398

commit v8 on v7

--- a/solution.py
+++ b/solution.py
@@ -13,7 +13,7 @@
 LAST = GROUPS - 1
 ZS = 8
 TILE = 512
-WIDE = 2048
+WIDE = 1024
 
 PEERS = (
     (0, 4), (1, 4), (0, 3), (0, 5), (1, 3), (1, 5), (0, 2), (0, 6),

time: 113 us -> 113 us (level)
  no operation moved by 1% of the time
where the time goes in v8:
time: 113 us; the launch traced here: 112 us
  Pallas kernels  111 us (98%)
    pallas_call x1, Pallas kernels, on_device(): pl.pallas_call(functools.partial(kernel, n_ex, n_mat), name='influence',...  109 us

profile of v8, /device:TPU:8, one launch (start us, length us, event | category | flops | bytes accessed | tf_op | source)
XLA Modules:
  0.0 111.8 jit_solution(8383630106680282883)
XLA Ops:
  0.6 109.0 %influence.1 = (bf16[16,64,2048]{2,1,0:T(8,128)(2,1)S(1)}, f32[3,16,256]{2,1,0:T(8,128)S(1)}, f32[2,16,128]{2,1,0:T(8,128)S(1)}, bf16[3,7,16,256]{3,2,1,0:T(8,128)(2,1)S(1)}, bf16[15,2,16,128]{3,2,1,0:T(8,128)(2,1)S(1)}) custom-call(bf16[1024,2048]{1,0:T(8,128)(2,1)} %bitcast.5, bf16[2048,2048]{1,0:T(8,128)(2,1)} %bitcast.4, bf16[16,2048]{1,0:T(8,128)(2,1)} %bitcast.7), custom_call_target="tpu_custom_call" | custom-call | flops 9663676416 | bytes 16777216 | tf_op jit(solution)/shard_map/influence/pallas_call | solution.py:346
  109.6 2.2 %write_out.1 = (bf16[16,64,2048]{2,1,0:T(8,128)(2,1)}, f32[16,1024]{1,0:T(8,128)}) custom-call(bf16[16,64,2048]{2,1,0:T(8,128)(2,1)S(1)} %get-tuple-element.9.pre_ref, f32[3,16,256]{2,1,0:T(8,128)S(1)} %get-tuple-element.10.own, f32[2,16,128]{2,1,0:T(8,128)S(1)} %get-tuple-element.11.own_last, bf16[3,7,16,256]{3,2,1,0:T(8,128)(2,1)S(1)} %get-tuple-element.12.z_in, ...), custom_call_target="tpu_custom_call" | custom-call | tf_op jit(solution)/shard_map/write_out/pallas_call | solution.py:398
